TPU v7x, 128 devices: a whole 4x4x4 slice. The times are simulated.
128 devices in a mesh: dp: 8 (over x, core), seq: 16 (over z, y).
Axes of the slice: x: 4, y: 4, z: 4, core: 2. Of those that a mesh axis runs over, the one named last changes fastest.
Arguments:
- trunk: bfloat16 [8, 4096, 1536], P('dp', 'seq'), may hold values from -34 to 34
- skip: bfloat16 [8, 8192, 1536], P('dp', 'seq'), may hold values from -6 to 6
- valid_bins: int32 [8], P('dp'), may hold values from 2048 to 4096, as said below
- query_weight: bfloat16 [1536, 256], replicated
- key_weight: bfloat16 [1536, 256], replicated
- value_weight: bfloat16 [1536, 768], replicated, may hold values from -0.15625 to 0.15625
- out_weight: bfloat16 [768, 1536], replicated, may hold values from -0.21875 to 0.21875
- depth_weight: float32 [3, 1536], replicated, may hold values from -3 to 3
- point_weight: bfloat16 [1536, 1536], replicated, may hold values from -0.15625 to 0.15625
- cotangent: bfloat16 [8, 8192, 1536], P('dp', 'seq'), may hold values from -6 to 6
Outputs:
- grad_pointwise: bfloat16 [1536, 1536], replicated
- grad_depthwise: float32 [3, 1536], replicated
- grad_skip: bfloat16 [8, 8192, 1536], P('dp', 'seq')
Inputs may be any that keep to these rules, and one draw needn't show every extreme that they name: Bins at or past a window's valid_bins are padding; in every draw some window is whole.
All inputs are finite; a program needn't handle non-finite values.
Results may differ from a plain program's by a relative error of at most 0.017.
Values may be sent and summed in bfloat16 or wider, within the bound.
No kernel may reach another device: no remote copies, remote signals or barrier semaphores. Data moves between devices by JAX's collectives and lax.ppermute only.
A program may use at most 128 MiB of HBM per device.

v0:
```python
from functools import partial
import math
import jax
import jax.numpy as jnp
from jax import lax
from jax.sharding import PartitionSpec as P

H = 4
DH = 64
DV = 192


def padded_2(cells, sides, width):
    for axis, dim in sides:
        count = lax.axis_size(axis)
        ends = count - 1
        head = lax.slice_in_dim(cells, 0, width, axis=dim)
        tail = lax.slice_in_dim(cells, cells.shape[dim] - width, cells.shape[dim], axis=dim)
        cells = jnp.concatenate(
            [
                lax.ppermute(tail, axis, [(i, (i + 1) % count) for i in range(ends)]),
                cells,
                lax.ppermute(head, axis, [((i + 1) % count, i) for i in range(ends)]),
            ],
            axis=dim,
        )
    return cells


def local(
    trunk,
    skip,
    valid_bins,
    query_weight,
    key_weight,
    value_weight,
    out_weight,
    depth_weight,
    point_weight,
    cotangent,
):
    tokens = trunk[0]
    row_count = tokens.shape[0]
    score_scale = 1.0 / math.sqrt(DH)
    queries = (
        jnp.dot(tokens, query_weight, preferred_element_type=jnp.float32)
        .astype(jnp.bfloat16)
        .reshape(row_count, H, DH)
    )
    keys = jnp.dot(tokens, key_weight, preferred_element_type=jnp.float32).astype(jnp.bfloat16)
    values = jnp.dot(tokens, value_weight, preferred_element_type=jnp.float32).astype(jnp.bfloat16)
    limit = valid_bins[0]
    running_max = jnp.full((H, row_count), -1e30, jnp.float32)
    weighted = jnp.zeros((row_count, H, DV), jnp.float32)
    key_piece = lax.all_gather(keys, "seq", axis=0, tiled=True)
    value_piece = lax.all_gather(values, "seq", axis=0, tiled=True)
    width = key_piece.shape[0]
    key_heads = key_piece.reshape(width, H, DH)
    value_heads = value_piece.reshape(width, H, DV)
    scores = (
        jnp.einsum("qhd,khd->hqk", queries, key_heads, preferred_element_type=jnp.float32)
        * score_scale
    )
    places = jnp.arange(width, dtype=jnp.int32)
    scores = jnp.where(places[None, None, :] < limit, scores, -1e30)
    fresh_max = jnp.maximum(running_max, jnp.max(scores, axis=2))
    shrink = jnp.exp(running_max - fresh_max)
    weights_raw = jnp.exp(scores - fresh_max[:, :, None])
    running_total = jnp.sum(weights_raw, axis=2)
    update = jnp.einsum(
        "hqk,khd->qhd",
        weights_raw.astype(jnp.bfloat16),
        value_heads,
        preferred_element_type=jnp.float32,
    )
    weighted = weighted * shrink.T[:, :, None] + update
    running_max, running_total, weighted = (fresh_max, running_total, weighted)
    mixed = (weighted / running_total.T[:, :, None]).reshape(row_count, H * DV)
    attended = (mixed * lax.rsqrt(jnp.mean(mixed * mixed, axis=1, keepdims=True) + 1e-05)).astype(
        jnp.bfloat16
    )
    hidden = (
        tokens.astype(jnp.float32)
        + jnp.dot(attended, out_weight, preferred_element_type=jnp.float32)
    ).astype(jnp.bfloat16)
    upsampled = (
        jnp.repeat(hidden, 2, axis=0).astype(jnp.float32) + skip[0].astype(jnp.float32)
    ).astype(jnp.bfloat16)
    padded = padded_2(upsampled, (("seq", 0),), 1)
    pre_act = (
        depth_weight[0] * padded[:-2]
        + depth_weight[1] * padded[1:-1]
        + depth_weight[2] * padded[2:]
    )
    act_value, pullback = jax.vjp(partial(jax.nn.gelu, approximate=True), pre_act)
    activated = act_value.astype(jnp.bfloat16)
    upstream = cotangent[0]
    grad_act = lax.dot_general(
        upstream, point_weight, (((1,), (1,)), ((), ())), preferred_element_type=jnp.float32
    )
    grad_pre = pullback(grad_act)[0].astype(jnp.bfloat16)
    fine_rows = grad_pre.shape[0]
    grad_wide = grad_pre.astype(jnp.float32)
    depth_term = jnp.stack(
        [
            jnp.sum(padded[offset : offset + fine_rows].astype(jnp.float32) * grad_wide, axis=0)
            for offset in range(3)
        ]
    )
    grad_padded = padded_2(grad_pre, (("seq", 0),), 1)
    grad_skip = (
        depth_weight[0] * grad_padded[2:]
        + depth_weight[1] * grad_padded[1:-1]
        + depth_weight[2] * grad_padded[:-2]
    ).astype(jnp.bfloat16)
    norm_scale = 1.0 / math.sqrt(lax.axis_size("dp") * lax.axis_size("seq") * fine_rows)
    point_term = lax.dot_general(
        activated, upstream, (((0,), (0,)), ((), ())), preferred_element_type=jnp.float32
    )
    point_total, depth_total = lax.psum((point_term, depth_term), ("dp", "seq"))
    grad_pointwise = (point_total * norm_scale).astype(jnp.bfloat16)
    return (grad_pointwise, depth_total * norm_scale, grad_skip[None])


def solution(mesh):
    return jax.shard_map(
        local,
        mesh=mesh,
        in_specs=(
            P("dp", "seq", None),
            P("dp", "seq", None),
            P("dp"),
            P(),
            P(),
            P(),
            P(),
            P(),
            P(),
            P("dp", "seq", None),
        ),
        out_specs=(P(), P(), P("dp", "seq", None)),
        check_vma=False,
    )
```

profile of v0, /device:TPU:1, one launch (start us, length us, event | category | flops | bytes accessed | tf_op | source)
XLA Modules:
  0.0 349.5 jit_solution(12524377417579679030)
XLA Ops:
  7.2 0.0 copy-start
  7.2 0.0 copy-start.3
  7.2 0.0 all-gather.3.cloned.1.call-start
  7.2 2.6 convolution_convert_fusion.1
  9.8 0.0 all-gather.3.cloned.1.call-update
  9.8 0.0 all-gather.5.cloned.1.call-start
  9.9 3.4 convolution_convert_fusion
  13.3 0.0 all-gather.5.cloned.1.call-update
  13.4 0.0 all-reduce.2.cloned.1.call-start
  14.1 0.0 copy-done.3
  14.1 1.6 convolution_convert_fusion.2
  15.7 42.6 %all-gather.3.cloned.1.call-done = bf16[4096,256]{1,0:T(8,128)(2,1)} async-done(((bf16[256,256]{1,0:T(8,128)(2,1)}), bf16[4096,256]{1,0:T(8,128)(2,1)}) %all-gather.3.cloned.1.call-update) | async-done | bytes 2097168 | tf_op jit(solution)/shard_map/all_gather | solution.py:55
  58.2 4.1 %copy.15 = bf16[4096,256]{0,1:T(8,128)(2,1)} copy(bf16[4096,256]{1,0:T(8,128)(2,1)} %all-gather.3.cloned.1.call-done) | data formatting | bytes 4194304 | tf_op jit(solution)/shard_map/all_gather | solution.py:55
  62.3 4.1 %fusion = (f32[4,256]{1,0:T(4,128)S(1)}, f32[4,256,4096]{2,1,0:T(8,128)S(1)}) fusion(pred[4096]{0:T(1024)(128)(4,1)S(1)} %iota_compare_fusion, bf16[256,4,64]{0,2,1:T(8,128)(2,1)S(1)} %bitcast.49, bf16[4096,4,64]{0,2,1:T(8,128)(2,1)} %bitcast.47), kind=kOutput, calls=%fused_computation.2 | convolution fusion | flops 549452800 | bytes 19013632 | tf_op jit(solution)/shard_map/qhd,khd->hqk/dot_general | solution.py:61
  66.4 0.0 copy-start.2
  66.4 5.9 %copy-done.2 = f32[4,256,4096]{2,1,0:T(8,128)} copy-done((f32[4,256,4096]{2,1,0:T(8,128)}, f32[4,256,4096]{2,1,0:T(8,128)S(1)}, u32[]{:S(2)}) %copy-start.2) | copy-done | bytes 16777240
  72.4 4.0 %fusion.1 = f32[4,256]{1,0:T(4,128)S(1)} fusion(f32[4,256,4096]{2,1,0:T(8,128)S(1)} %get-tuple-element.17, f32[4,256]{1,0:T(4,128)S(1)} %get-tuple-element.15, pred[4096]{0:T(1024)(128)(4,1)S(1)} %iota_compare_fusion), kind=kLoop, calls=%fused_computation.3 | loop fusion | flops 16776192 | bytes 16789504 | tf_op jit(solution)/shard_map/reduce_sum | solution.py:69
  76.4 46.3 %all-gather.5.cloned.1.call-done = bf16[4096,768]{1,0:T(8,128)(2,1)} async-done(((bf16[256,768]{1,0:T(8,128)(2,1)}), bf16[4096,768]{1,0:T(8,128)(2,1)}) %all-gather.5.cloned.1.call-update) | async-done | bytes 6291472 | tf_op jit(solution)/shard_map/all_gather | solution.py:56
  122.7 8.6 %copy.16 = bf16[4096,768]{0,1:T(8,128)(2,1)} copy(bf16[4096,768]{1,0:T(8,128)(2,1)} %all-gather.5.cloned.1.call-done) | data formatting | bytes 12582912 | tf_op jit(solution)/shard_map/all_gather | solution.py:56
  131.3 10.3 %multiply_reduce_fusion = (f32[256]{0:T(256)S(1)}, f32[256,4,192]{0,2,1:T(8,128)S(1)}) fusion(f32[256,4]{0,1:T(4,128)S(1)} %bitcast.50, bf16[4096,4,192]{0,2,1:T(8,128)(2,1)} %bitcast.48, f32[4,256,4096]{2,1,0:T(8,128)} %copy-done.2, f32[4,256]{1,0:T(4,128)S(1)} %get-tuple-element.15, pred[4096]{0:T(1024)(128)(4,1)S(1)} %iota_compare_fusion, ...), kind=kOutput, calls=%fused_computation.68 | convolution fusion | flops 1628176128 | bytes 23872512 | tf_op jit(solution)/shard_map/hqk,khd->qhd/dot_general | solution.py:70
  141.6 0.1 fusion.51
  141.7 0.0 copy-done
  141.7 0.8 fusion.26
  142.5 2.7 broadcast_in_dim.33
  145.2 5.2 %convert_element_type.79 = f32[512,1536]{1,0:T(8,128)} reshape(f32[256,2,1536]{2,1,0:T(2,128)} %broadcast_in_dim.33) | data formatting | bytes 6291456 | tf_op jit(solution)/shard_map/convert_element_type | solution.py:87
  150.5 0.0 copy-start.4
  150.5 0.0 copy-start.5
  150.5 2.9 fusion.24
  153.4 3.1 collective-permute-start
  156.6 1.5 collective-permute-start.1
  158.0 0.0 copy-done.4
  158.0 0.1 slice_reduce_fusion.2
  158.1 0.0 collective-permute-done
  158.1 2.8 collective-permute-done.1
  160.9 0.0 copy-done.5
  160.9 6.6 %fusion.27 = f32[1536,1536]{1,0:T(8,128)} fusion(bf16[512,1536]{1,0:T(8,128)(2,1)S(1)} %fusion.24, bf16[1,1536]{1,0:T(2,128)(2,1)S(1)} %collective-permute-done.1, bf16[1,1536]{1,0:T(2,128)(2,1)S(1)} %collective-permute-done, bf16[1,512,1536]{2,1,0:T(8,128)(2,1)S(1)} %copy-done.5, f32[1536]{0:T(1024)S(1)} %get-tuple-element.7, ...), kind=kOutput, calls=%fused_computation.41 | convolution fusion | flops 2434007040 | bytes 12607488 | tf_op jit(solution)/shard_map/dot_general | solution.py:117
  167.5 0.0 all-reduce.2.cloned.1.call-update
  167.5 7.5 %fusion.17 = bf16[512,1536]{1,0:T(8,128)(2,1)S(1)} fusion(bf16[1,1536]{1,0:T(2,128)(2,1)S(1)} %collective-permute-done.1, bf16[512,1536]{1,0:T(8,128)(2,1)S(1)} %fusion.24, bf16[1,1536]{1,0:T(2,128)(2,1)S(1)} %collective-permute-done, bf16[1536,1536]{1,0:T(8,128)(2,1)} %param.18, bf16[1,512,1536]{2,1,0:T(8,128)(2,1)} %param.19, ...), kind=kOutput, calls=%fused_computation.28 | convolution fusion | flops 2442657792 | bytes 9461760 | tf_op jit(solution)/shard_map/dot_general | solution.py:98
  175.1 1.3 collective-permute-start.2
  176.4 4.0 %collective-permute-start.3 = (bf16[1,1536]{1,0:T(2,128)(2,1)S(1)}, bf16[1,1536]{1,0:T(2,128)(2,1)S(1)}, u32[]{:S(2)}, u32[]{:S(2)}) collective-permute-start(bf16[1,1536]{1,0:T(2,128)(2,1)S(1)} %get-tuple-element.11), channel_id=1, source_target_pairs={{0,1},{1,2},{2,3},{3,4},{4,5},{5,6},{6,7},{7,8},{8,9},{9,10},{10,1... | collective-permute-start | bytes 9224 | tf_op jit(solution)/shard_map/ppermute | solution.py:21
  180.4 0.0 collective-permute-done.2
  180.4 0.7 collective-permute-done.3
  181.1 3.5 %fusion.18 = (f32[1536]{0:T(1024)S(1)}, f32[1536]{0:T(1024)S(1)}, f32[1536]{0:T(1024)S(1)}, bf16[1,512,1536]{2,1,0:T(8,128)(2,1)}) fusion(bf16[512,1536]{1,0:T(8,128)(2,1)S(1)} %fusion.17, bf16[512,1536]{1,0:T(8,128)(2,1)S(1)} %fusion.24, bf16[1,1536]{1,0:T(2,128)(2,1)S(1)} %collective-permute-done, bf16[1,1536]{1,0:T(2,128)(2,1)S(1)} %collective-permute-done.1, ...), kind=kLoop, calls=%fused_computation.29 | loop fusion | flops 23588352 | bytes 4767744 | tf_op jit(solution)/shard_map/reduce_sum | solution.py:106
  184.7 74.9 %psum.15 = f32[3,1536]{1,0:T(4,128)S(1)} all-reduce(f32[3,1536]{1,0:T(4,128)S(1)} %pad_maximum_fusion.5), channel_id=1, replica_groups=mesh['dp'=8,'seq'=16] {'dp','seq'}, use_global_device_ids=true, to_apply=%region_7.8 | all-reduce | flops 4608 | bytes 36864 | tf_op jit(solution)/shard_map/psum | solution.py:120
  259.6 0.6 broadcast_multiply_fusion
  260.2 75.5 %all-reduce.2.cloned.1.call-done = f32[1536,1536]{1,0:T(8,128)} async-done(((f32[1536,1536]{1,0:T(8,128)}), f32[1536,1536]{1,0:T(8,128)}) %all-reduce.2.cloned.1.call-update) | async-done | bytes 9437200 | tf_op jit(solution)/shard_map/psum | solution.py:120
  335.7 7.2 %multiply_convert_fusion = bf16[1536,1536]{1,0:T(8,128)(2,1)} fusion(f32[1536,1536]{1,0:T(8,128)} %all-reduce.2.cloned.1.call-done), kind=kLoop, calls=%fused_computation.5 | loop fusion | flops 4718592 | bytes 14155776 | tf_op jit(solution)/shard_map/convert_element_type | solution.py:121
  343.0 0.0 copy-done.1
  (10 shorter events, 0.1 us)
Async XLA Ops:
  7.2 134.5 %copy-start = (bf16[768,1536]{1,0:T(8,128)(2,1)S(1)}, bf16[768,1536]{1,0:T(8,128)(2,1)}, u32[]{:S(2)}) copy-start(bf16[768,1536]{1,0:T(8,128)(2,1)} %param.16) | copy-start | bytes 7077892
  7.2 6.9 %copy-start.3 = (bf16[1,256,1536]{2,1,0:T(8,128)(2,1)S(1)}, bf16[1,256,1536]{2,1,0:T(8,128)(2,1)}, u32[]{:S(2)}) copy-start(bf16[1,256,1536]{2,1,0:T(8,128)(2,1)} %param.10) | copy-start | bytes 2359300
  7.2 51.0 %all-gather.3.cloned.1.call-start = ((), (), s32[]{:S(2)}) async-start(), calls=%async_computation | async-start | bytes 2228224 | tf_op jit(solution)/shard_map/all_gather | solution.py:55
  9.8 112.8 %all-gather.5.cloned.1.call-start = ((), (), s32[]{:S(2)}) async-start(), calls=%async_computation.1 | async-start | bytes 6684672 | tf_op jit(solution)/shard_map/all_gather | solution.py:56
  13.4 322.4 %all-reduce.2.cloned.1.call-start = ((), (), s32[]{:S(2)}) async-start(), calls=%async_computation.2 | async-start | bytes 18874368 | tf_op jit(solution)/shard_map/psum | solution.py:120
  66.4 6.0 %copy-start.2 = (f32[4,256,4096]{2,1,0:T(8,128)}, f32[4,256,4096]{2,1,0:T(8,128)S(1)}, u32[]{:S(2)}) copy-start(f32[4,256,4096]{2,1,0:T(8,128)S(1)} %get-tuple-element.17) | copy-start | bytes 50331652
  150.5 7.6 %copy-start.4 = (f32[3,1536]{1,0:T(4,128)S(1)}, f32[3,1536]{1,0:T(4,128)}, u32[]{:S(2)}) copy-start(f32[3,1536]{1,0:T(4,128)} %param.17) | copy-start | bytes 55300
  150.5 10.4 %copy-start.5 = (bf16[1,512,1536]{2,1,0:T(8,128)(2,1)S(1)}, bf16[1,512,1536]{2,1,0:T(8,128)(2,1)}, u32[]{:S(2)}) copy-start(bf16[1,512,1536]{2,1,0:T(8,128)(2,1)} %param.19) | copy-start | bytes 4718596
  153.4 4.7 %collective-permute-start = (bf16[1,1536]{1,0:T(2,128)(2,1)S(1)}, bf16[1,1536]{1,0:T(2,128)(2,1)S(1)}, u32[]{:S(2)}, u32[]{:S(2)}) collective-permute-start(bf16[1,1536]{1,0:T(2,128)(2,1)S(1)} %get-tuple-element.12), channel_id=1, source_target_pairs={{0,1},{1,2},{2,3},{3,4},{4,5},{5,6},{6,7},{7,8},{8,9},{9,10},{10,1... | collective-permute-start | bytes 9224 | tf_op jit(solution)/shard_map/ppermute | solution.py:21
  156.6 4.4 %collective-permute-start.1 = (bf16[1,1536]{1,0:T(2,128)(2,1)S(1)}, bf16[1,1536]{1,0:T(2,128)(2,1)S(1)}, u32[]{:S(2)}, u32[]{:S(2)}) collective-permute-start(bf16[1,1536]{1,0:T(2,128)(2,1)S(1)} %get-tuple-element.13), channel_id=1, source_target_pairs={{1,0},{2,1},{3,2},{4,3},{5,4},{6,5},{7,6},{8,7},{9,8},{10,9},{11,1... | collective-permute-start | bytes 9224 | tf_op jit(solution)/shard_map/ppermute | solution.py:23
  175.1 5.3 %collective-permute-start.2 = (bf16[1,1536]{1,0:T(2,128)(2,1)S(1)}, bf16[1,1536]{1,0:T(2,128)(2,1)S(1)}, u32[]{:S(2)}, u32[]{:S(2)}) collective-permute-start(bf16[1,1536]{1,0:T(2,128)(2,1)S(1)} %get-tuple-element.10), channel_id=1, source_target_pairs={{1,0},{2,1},{3,2},{4,3},{5,4},{6,5},{7,6},{8,7},{9,8},{10,9},{11,1... | collective-permute-start | bytes 9224 | tf_op jit(solution)/shard_map/ppermute | solution.py:23
  176.4 4.8 %collective-permute-start.3 = (bf16[1,1536]{1,0:T(2,128)(2,1)S(1)}, bf16[1,1536]{1,0:T(2,128)(2,1)S(1)}, u32[]{:S(2)}, u32[]{:S(2)}) collective-permute-start(bf16[1,1536]{1,0:T(2,128)(2,1)S(1)} %get-tuple-element.11), channel_id=1, source_target_pairs={{0,1},{1,2},{2,3},{3,4},{4,5},{5,6},{6,7},{7,8},{8,9},{9,10},{10,1... | collective-permute-start | bytes 9224 | tf_op jit(solution)/shard_map/ppermute | solution.py:21
  335.7 7.2 %copy-start.1 = (bf16[768,1536]{1,0:T(8,128)(2,1)S(1)}, bf16[768,1536]{1,0:T(8,128)(2,1)}, u32[]{:S(2)}) copy-start(bf16[768,1536]{1,0:T(8,128)(2,1)} %param.16) | copy-start | bytes 7077892
Sparse Core Ops, SparseCore 0:
  10.7 47.4 all-gather.2
  60.9 61.6 all-gather.4
  167.6 168.0 all-reduce.1
where the time goes:
time: 350 us
  waiting for transfers between devices  168 us (48%)
  blocking collectives  74.9 us (21%)
  matrix products  36.9 us (11%)
  local copies, waits for them, and re-layouts  26.7 us (8%)
  other arithmetic  18.4 us (5%)
  between operations  14.6 us (4%)
  starting transfers between devices  9.98 us (3%)
    psum x1, waiting for transfers between devices, local(): point_total, depth_total = lax.psum((point_term, depth_term), ('dp', 'seq'))  75.5 us
    psum x1, blocking collectives, local(): point_total, depth_total = lax.psum((point_term, depth_term), ('dp', 'seq'))  74.9 us
    all_gather x1, waiting for transfers between devices, local(): value_piece = lax.all_gather(values, 'seq', axis=0, tiled=True)  46.3 us
    all_gather x1, waiting for transfers between devices, local(): key_piece = lax.all_gather(keys, 'seq', axis=0, tiled=True)  42.6 us
    dot_general x1, matrix products, local(): jnp.einsum('hqk,khd->qhd', weights_raw.astype(jnp.bfloat16), value_heads,...  10.3 us
    all_gather x1, local copies, waits for them, and re-layouts, local(): value_piece = lax.all_gather(values, 'seq', axis=0, tiled=True)  8.63 us
    dot_general x1, matrix products, local(): lax.dot_general(upstream, point_weight, (((1,), (1,)), ((), ())), preferr...  7.54 us
    convert_element_type x1, other arithmetic, local(): grad_pointwise = (point_total * norm_scale).astype(jnp.bfloat16)  7.24 us
  transfers between devices with their start and end apart: 7, of which 5 were waited for; matrix products, arithmetic and copies ran while one was open for 8% of the time, Pallas kernels for 0%

commit v1 on v0

--- a/solution.py
+++ b/solution.py
@@ -52,8 +52,11 @@
     limit = valid_bins[0]
     running_max = jnp.full((H, row_count), -1e30, jnp.float32)
     weighted = jnp.zeros((row_count, H, DV), jnp.float32)
-    key_piece = lax.all_gather(keys, "seq", axis=0, tiled=True)
-    value_piece = lax.all_gather(values, "seq", axis=0, tiled=True)
+    key_piece, value_piece = jnp.split(
+        lax.all_gather(jnp.concatenate([keys, values], 1), "seq", axis=0, tiled=True),
+        [keys.shape[1]],
+        1,
+    )
     width = key_piece.shape[0]
     key_heads = key_piece.reshape(width, H, DH)
     value_heads = value_piece.reshape(width, H, DV)

time: 350 us -> 338 us (0.966)
  waiting for transfers between devices: 168 us -> 151 us
  local copies, waits for them, and re-layouts: 26.7 us -> 31.7 us
    split x0 -> x4, local copies, waits for them, and re-layouts: none -> 21.8 us  [local(): jnp.split(lax.all_gather(jnp.concatenate([keys, values], 1), 'seq', axis=...]
    all_gather x2 -> x1, waiting for transfers between devices: 88.9 us -> 72 us  [local(): lax.all_gather(jnp.concatenate([keys, values], 1), 'seq', axis=0, tiled=T...]
    all_gather x2 -> x0, local copies, waits for them, and re-layouts: 12.7 us -> none  [the longest x1 8.63 us: local(): value_piece = lax.all_gather(values, 'seq', axis=0, tiled=True)]
    unnamed x12, local copies, waits for them, and re-layouts: 5.96 us -> 1.69 us
  transfers between devices with their start and end apart: 7 -> 6, of which waited for: 5 -> 4; matrix products, arithmetic and copies ran while one was open for 8% -> 4% of each run, Pallas kernels for 0% -> 0%
where the time goes in v1:
time: 338 us; the launch traced here: 337 us
  waiting for transfers between devices  151 us (45%)
  blocking collectives  74.9 us (22%)
  matrix products  35.5 us (11%)
  local copies, waits for them, and re-layouts  31.7 us (9%)
  other arithmetic  19.3 us (6%)
  between operations  14.9 us (4%)
  starting transfers between devices  9.94 us (3%)
    psum x1, waiting for transfers between devices, local(): point_total, depth_total = lax.psum((point_term, depth_term), ('dp', 'seq'))  75.5 us
    psum x1, blocking collectives, local(): point_total, depth_total = lax.psum((point_term, depth_term), ('dp', 'seq'))  74.9 us
    all_gather x1, waiting for transfers between devices, local(): lax.all_gather(jnp.concatenate([keys, values], 1), 'seq', axis=0, tiled=T...  72 us
    split x4, local copies, waits for them, and re-layouts, local(): jnp.split(lax.all_gather(jnp.concatenate([keys, values], 1), 'seq', axis=...  21.8 us
    dot_general x1, matrix products, local(): jnp.einsum('hqk,khd->qhd', weights_raw.astype(jnp.bfloat16), value_heads,...  10.3 us
    dot_general x1, matrix products, local(): lax.dot_general(upstream, point_weight, (((1,), (1,)), ((), ())), preferr...  7.54 us
    convert_element_type x1, other arithmetic, local(): grad_pointwise = (point_total * norm_scale).astype(jnp.bfloat16)  7.24 us
    ppermute x2, starting transfers between devices, padded_2(): lax.ppermute(tail, axis, [(i, (i + 1) % count) for i in range(ends)])  7.1 us
  transfers between devices with their start and end apart: 6, of which 4 were waited for; matrix products, arithmetic and copies ran while one was open for 4% of the time, Pallas kernels for 0%

profile of v1, /device:TPU:1, one launch (start us, length us, event | category | flops | bytes accessed | tf_op | source)
XLA Modules:
  0.0 337.3 jit_solution(5054450176500487343)
XLA Ops:
  7.2 0.0 copy-start
  7.2 0.0 all-gather.2.cloned.1.call-start
  7.2 1.9 convolution_convert_fusion.1
  9.2 0.0 copy-start.3
  9.2 0.1 copy.16
  9.3 2.7 convolution_convert_fusion
  12.0 0.9 pad_maximum_fusion.5
  12.9 0.0 all-gather.2.cloned.1.call-update
  12.9 0.0 all-reduce.2.cloned.1.call-start
  13.6 0.0 copy-done.3
  13.6 1.6 convolution_convert_fusion.2
  15.2 72.0 %all-gather.2.cloned.1.call-done = bf16[4096,1024]{1,0:T(8,128)(2,1)} async-done(((bf16[256,1024]{1,0:T(8,128)(2,1)}), bf16[4096,1024]{1,0:T(8,128)(2,1)}) %all-gather.2.cloned.1.call-update) | async-done | bytes 8388624 | tf_op jit(solution)/shard_map/all_gather | solution.py:56
  87.2 5.9 %split.9 = bf16[4096,768]{1,0:T(8,128)(2,1)} slice(bf16[4096,1024]{1,0:T(8,128)(2,1)} %all-gather.2.cloned.1.call-done), slice={[0:4096], [256:1024]} | slice | bytes 12582912 | tf_op jit(solution)/shard_map/split | solution.py:55
  93.1 8.8 %copy.18 = bf16[4096,768]{0,1:T(8,128)(2,1)} copy(bf16[4096,768]{1,0:T(8,128)(2,1)} %split.9) | data formatting | bytes 12582912 | tf_op jit(solution)/shard_map/split | solution.py:55
  101.8 3.0 split.8
  104.9 4.1 %copy.17 = bf16[4096,256]{0,1:T(8,128)(2,1)} copy(bf16[4096,256]{1,0:T(8,128)(2,1)} %split.8) | data formatting | bytes 4194304 | tf_op jit(solution)/shard_map/split | solution.py:55
  109.0 4.1 %fusion = (f32[4,256]{1,0:T(4,128)S(1)}, f32[4,256,4096]{2,1,0:T(8,128)S(1)}) fusion(pred[4096]{0:T(1024)(128)(4,1)S(1)} %iota_compare_fusion, bf16[256,4,64]{0,2,1:T(8,128)(2,1)S(1)} %bitcast.49, bf16[4096,4,64]{0,2,1:T(8,128)(2,1)} %bitcast.47), kind=kOutput, calls=%fused_computation.2 | convolution fusion | flops 549452800 | bytes 19013632 | tf_op jit(solution)/shard_map/qhd,khd->hqk/dot_general | solution.py:64
  113.1 0.0 copy-start.2
  113.1 4.0 %fusion.1 = f32[4,256]{1,0:T(4,128)S(1)} fusion(f32[4,256,4096]{2,1,0:T(8,128)S(1)} %get-tuple-element.17, f32[4,256]{1,0:T(4,128)S(1)} %get-tuple-element.15, pred[4096]{0:T(1024)(128)(4,1)S(1)} %iota_compare_fusion), kind=kLoop, calls=%fused_computation.3 | loop fusion | flops 16776192 | bytes 16789504 | tf_op jit(solution)/shard_map/reduce_sum | solution.py:72
  117.2 1.7 copy-done.2
  118.8 10.3 %multiply_reduce_fusion = (f32[256]{0:T(256)S(1)}, f32[256,4,192]{0,2,1:T(8,128)S(1)}) fusion(f32[256,4]{0,1:T(4,128)S(1)} %bitcast.50, bf16[4096,4,192]{0,2,1:T(8,128)(2,1)} %bitcast.48, f32[4,256,4096]{2,1,0:T(8,128)} %copy-done.2, f32[4,256]{1,0:T(4,128)S(1)} %get-tuple-element.15, pred[4096]{0:T(1024)(128)(4,1)S(1)} %iota_compare_fusion, ...), kind=kOutput, calls=%fused_computation.68 | convolution fusion | flops 1628176128 | bytes 23872512 | tf_op jit(solution)/shard_map/hqk,khd->qhd/dot_general | solution.py:73
  129.1 0.1 fusion.51
  129.2 0.0 copy-done
  129.2 0.8 fusion.26
  130.0 2.7 broadcast_in_dim.33
  132.7 5.2 %convert_element_type.79 = f32[512,1536]{1,0:T(8,128)} reshape(f32[256,2,1536]{2,1,0:T(2,128)} %broadcast_in_dim.33) | data formatting | bytes 6291456 | tf_op jit(solution)/shard_map/convert_element_type | solution.py:90
  138.0 0.0 copy-start.4
  138.0 2.9 fusion.24
  140.9 3.1 collective-permute-start
  144.1 1.5 collective-permute-start.1
  145.5 0.0 copy-done.4
  145.5 0.1 slice_reduce_fusion.2
  145.6 0.0 collective-permute-done
  145.6 2.8 collective-permute-done.1
  148.4 0.0 copy-done.5
  148.4 6.6 %fusion.27 = f32[1536,1536]{1,0:T(8,128)} fusion(bf16[512,1536]{1,0:T(8,128)(2,1)S(1)} %fusion.24, bf16[1,1536]{1,0:T(2,128)(2,1)S(1)} %collective-permute-done.1, bf16[1,1536]{1,0:T(2,128)(2,1)S(1)} %collective-permute-done, bf16[1,512,1536]{2,1,0:T(8,128)(2,1)S(1)} %copy-done.5, f32[1536]{0:T(1024)S(1)} %get-tuple-element.7, ...), kind=kOutput, calls=%fused_computation.41 | convolution fusion | flops 2434007040 | bytes 12607488 | tf_op jit(solution)/shard_map/dot_general | solution.py:120
  155.0 0.0 all-reduce.2.cloned.1.call-update
  155.0 7.5 %fusion.17 = bf16[512,1536]{1,0:T(8,128)(2,1)S(1)} fusion(bf16[1,1536]{1,0:T(2,128)(2,1)S(1)} %collective-permute-done.1, bf16[512,1536]{1,0:T(8,128)(2,1)S(1)} %fusion.24, bf16[1,1536]{1,0:T(2,128)(2,1)S(1)} %collective-permute-done, bf16[1536,1536]{1,0:T(8,128)(2,1)} %param.18, bf16[1,512,1536]{2,1,0:T(8,128)(2,1)} %param.19, ...), kind=kOutput, calls=%fused_computation.28 | convolution fusion | flops 2442657792 | bytes 9461760 | tf_op jit(solution)/shard_map/dot_general | solution.py:101
  162.6 1.3 collective-permute-start.2
  163.9 4.0 %collective-permute-start.3 = (bf16[1,1536]{1,0:T(2,128)(2,1)S(1)}, bf16[1,1536]{1,0:T(2,128)(2,1)S(1)}, u32[]{:S(2)}, u32[]{:S(2)}) collective-permute-start(bf16[1,1536]{1,0:T(2,128)(2,1)S(1)} %get-tuple-element.11), channel_id=1, source_target_pairs={{0,1},{1,2},{2,3},{3,4},{4,5},{5,6},{6,7},{7,8},{8,9},{9,10},{10,1... | collective-permute-start | bytes 9224 | tf_op jit(solution)/shard_map/ppermute | solution.py:21
  167.9 0.0 collective-permute-done.2
  167.9 0.7 collective-permute-done.3
  168.7 3.5 %fusion.18 = (f32[1536]{0:T(1024)S(1)}, f32[1536]{0:T(1024)S(1)}, f32[1536]{0:T(1024)S(1)}, bf16[1,512,1536]{2,1,0:T(8,128)(2,1)}) fusion(bf16[512,1536]{1,0:T(8,128)(2,1)S(1)} %fusion.17, bf16[512,1536]{1,0:T(8,128)(2,1)S(1)} %fusion.24, bf16[1,1536]{1,0:T(2,128)(2,1)S(1)} %collective-permute-done, bf16[1,1536]{1,0:T(2,128)(2,1)S(1)} %collective-permute-done.1, ...), kind=kLoop, calls=%fused_computation.29 | loop fusion | flops 23588352 | bytes 4767744 | tf_op jit(solution)/shard_map/reduce_sum | solution.py:109
  172.2 74.9 %psum.15 = f32[3,1536]{1,0:T(4,128)S(1)} all-reduce(f32[3,1536]{1,0:T(4,128)S(1)} %pad_maximum_fusion.6), channel_id=1, replica_groups=mesh['dp'=8,'seq'=16] {'dp','seq'}, use_global_device_ids=true, to_apply=%region_7.8 | all-reduce | flops 4608 | bytes 36864 | tf_op jit(solution)/shard_map/psum | solution.py:123
  247.1 0.6 broadcast_multiply_fusion
  247.7 75.5 %all-reduce.2.cloned.1.call-done = f32[1536,1536]{1,0:T(8,128)} async-done(((f32[1536,1536]{1,0:T(8,128)}), f32[1536,1536]{1,0:T(8,128)}) %all-reduce.2.cloned.1.call-update) | async-done | bytes 9437200 | tf_op jit(solution)/shard_map/psum | solution.py:123
  323.3 7.2 %multiply_convert_fusion = bf16[1536,1536]{1,0:T(8,128)(2,1)} fusion(f32[1536,1536]{1,0:T(8,128)} %all-reduce.2.cloned.1.call-done), kind=kLoop, calls=%fused_computation.5 | loop fusion | flops 4718592 | bytes 14155776 | tf_op jit(solution)/shard_map/convert_element_type | solution.py:124
  330.5 0.0 copy-done.1
  (11 shorter events, 0.1 us)
Async XLA Ops:
  7.2 122.0 %copy-start = (bf16[768,1536]{1,0:T(8,128)(2,1)S(1)}, bf16[768,1536]{1,0:T(8,128)(2,1)}, u32[]{:S(2)}) copy-start(bf16[768,1536]{1,0:T(8,128)(2,1)} %param.16) | copy-start | bytes 7077892
  7.2 80.0 %all-gather.2.cloned.1.call-start = ((), (), s32[]{:S(2)}) async-start(), calls=%async_computation | async-start | bytes 8912896 | tf_op jit(solution)/shard_map/all_gather | solution.py:56
  9.2 4.5 %copy-start.3 = (bf16[1,256,1536]{2,1,0:T(8,128)(2,1)S(1)}, bf16[1,256,1536]{2,1,0:T(8,128)(2,1)}, u32[]{:S(2)}) copy-start(bf16[1,256,1536]{2,1,0:T(8,128)(2,1)} %param.10) | copy-start | bytes 2359300
  12.9 310.3 %all-reduce.2.cloned.1.call-start = ((), (), s32[]{:S(2)}) async-start(), calls=%async_computation.1 | async-start | bytes 18874368 | tf_op jit(solution)/shard_map/psum | solution.py:123
  113.1 5.7 %copy-start.2 = (f32[4,256,4096]{2,1,0:T(8,128)}, f32[4,256,4096]{2,1,0:T(8,128)S(1)}, u32[]{:S(2)}) copy-start(f32[4,256,4096]{2,1,0:T(8,128)S(1)} %get-tuple-element.17) | copy-start | bytes 50331652
  138.0 7.6 %copy-start.4 = (f32[3,1536]{1,0:T(4,128)S(1)}, f32[3,1536]{1,0:T(4,128)}, u32[]{:S(2)}) copy-start(f32[3,1536]{1,0:T(4,128)} %param.17) | copy-start | bytes 55300
  138.0 10.4 %copy-start.5 = (bf16[1,512,1536]{2,1,0:T(8,128)(2,1)S(1)}, bf16[1,512,1536]{2,1,0:T(8,128)(2,1)}, u32[]{:S(2)}) copy-start(bf16[1,512,1536]{2,1,0:T(8,128)(2,1)} %param.19) | copy-start | bytes 4718596
  140.9 4.7 %collective-permute-start = (bf16[1,1536]{1,0:T(2,128)(2,1)S(1)}, bf16[1,1536]{1,0:T(2,128)(2,1)S(1)}, u32[]{:S(2)}, u32[]{:S(2)}) collective-permute-start(bf16[1,1536]{1,0:T(2,128)(2,1)S(1)} %get-tuple-element.12), channel_id=1, source_target_pairs={{0,1},{1,2},{2,3},{3,4},{4,5},{5,6},{6,7},{7,8},{8,9},{9,10},{10,1... | collective-permute-start | bytes 9224 | tf_op jit(solution)/shard_map/ppermute | solution.py:21
  144.1 4.4 %collective-permute-start.1 = (bf16[1,1536]{1,0:T(2,128)(2,1)S(1)}, bf16[1,1536]{1,0:T(2,128)(2,1)S(1)}, u32[]{:S(2)}, u32[]{:S(2)}) collective-permute-start(bf16[1,1536]{1,0:T(2,128)(2,1)S(1)} %get-tuple-element.13), channel_id=1, source_target_pairs={{1,0},{2,1},{3,2},{4,3},{5,4},{6,5},{7,6},{8,7},{9,8},{10,9},{11,1... | collective-permute-start | bytes 9224 | tf_op jit(solution)/shard_map/ppermute | solution.py:23
  162.6 5.3 %collective-permute-start.2 = (bf16[1,1536]{1,0:T(2,128)(2,1)S(1)}, bf16[1,1536]{1,0:T(2,128)(2,1)S(1)}, u32[]{:S(2)}, u32[]{:S(2)}) collective-permute-start(bf16[1,1536]{1,0:T(2,128)(2,1)S(1)} %get-tuple-element.10), channel_id=1, source_target_pairs={{1,0},{2,1},{3,2},{4,3},{5,4},{6,5},{7,6},{8,7},{9,8},{10,9},{11,1... | collective-permute-start | bytes 9224 | tf_op jit(solution)/shard_map/ppermute | solution.py:23
  163.9 4.8 %collective-permute-start.3 = (bf16[1,1536]{1,0:T(2,128)(2,1)S(1)}, bf16[1,1536]{1,0:T(2,128)(2,1)S(1)}, u32[]{:S(2)}, u32[]{:S(2)}) collective-permute-start(bf16[1,1536]{1,0:T(2,128)(2,1)S(1)} %get-tuple-element.11), channel_id=1, source_target_pairs={{0,1},{1,2},{2,3},{3,4},{4,5},{5,6},{6,7},{7,8},{8,9},{9,10},{10,1... | collective-permute-start | bytes 9224 | tf_op jit(solution)/shard_map/ppermute | solution.py:21
  323.3 7.2 %copy-start.1 = (bf16[768,1536]{1,0:T(8,128)(2,1)S(1)}, bf16[768,1536]{1,0:T(8,128)(2,1)}, u32[]{:S(2)}) copy-start(bf16[768,1536]{1,0:T(8,128)(2,1)} %param.16) | copy-start | bytes 7077892
Sparse Core Ops, SparseCore 0:
  13.0 74.0 all-gather.1
  155.2 168.0 all-reduce.1
